TPU v7x, 32 devices: a whole 2x2x4 slice. The times are simulated.
32 devices in a mesh: groups: 2 (over y), lat: 4 (over z), slc: 2 (over x), rep: 2 (over core).
Axes of the slice: x: 2, y: 2, z: 4, core: 2. Of those that a mesh axis runs over, the one named last changes fastest.
Arguments:
- atom_xy: float32 [8, 2, 2, 256], P(('groups', 'lat'), 'slc'), parts along dimension 0, may hold values from 0 to 4096, as said below
- atom_species: int32 [8, 2, 256], P(('groups', 'lat'), 'slc'), parts along dimension 0, may hold values from 0 to 7
- atom_slab: int32 [8, 2, 256], P(('groups', 'lat'), 'slc'), parts along dimension 0, may hold values from 0 to 1
- species_amp: float32 [8], replicated, may hold values from 0.5 to 3
- species_spread: float32 [8], replicated, may hold values from 2 to 6
- margin: int32 [8, 2, 2, 2, 3, 128], P(('groups', 'lat'), 'slc', None, 'rep'), parts along dimension 0, may hold values from -1 to 255, as said below
- probe_pos: int32 [64, 2], P(('groups', 'lat', 'slc', 'rep')), parts along dimension 0, may hold values from 0 to 4092, as said below
Outputs:
- exit_wave: bfloat16 [64, 256, 2, 256], P(('groups', 'lat', 'slc', 'rep')), parts along dimension 0
There are 2 independent parts, one for each index of `groups`. A program takes and returns all parts, laid end to end along the dimension named above; an argument that names none is the same for every part. Nothing has to cross between parts.
Inputs may be any that keep to these rules, and one draw needn't show every extreme that they name: `atom_xy`: atom a of tile v has x between (v * 256 + a) b and (v * 256 + a + 1) b with b = 4, and y in [0, 256). `probe_pos`: the 2 probes of one lateral index, slice owner and rep index share their x anchor; the centre of each window lies in tile t, x is a multiple of 4 taken modulo 4096, and y is below 256. `margin`: each block lists a run of consecutive local atom indices in rising order, then -1: the atoms of tile v whose x lies within 128 pixels of the probes' windows (x modulo 4096).
All inputs are finite; a program needn't handle non-finite values.
Results may differ from a plain program's by a relative error of at most 0.03.
Values may be sent and summed in bfloat16 or wider, within the bound.
A program may use at most 128 MiB of HBM per device.

v0:
```python
import functools
import math

import jax
import jax.numpy as jnp
import ml_dtypes
import numpy as np
from jax import lax
from jax.experimental import pallas as pl
from jax.experimental.pallas import tpu as pltpu
from jax.sharding import PartitionSpec as P

PROPAGATION_COEF = 0.001
DEFOCUS_COEF = 4.19
LOG2E = math.log2(math.e)
MESH = pl.DeviceIdType.MESH

LANES = 128


def real_basis(window):
    top = max(k for k in range(window // 2) if 9 * k * k < window * window)
    freq = np.concatenate([np.arange(top + 1), np.arange(1, top + 1)])
    pixel = np.arange(window)
    angle = 2.0 * np.pi / window * (pixel[:, None] * freq[None, :] % window)
    basis = np.where(np.arange(freq.size) <= top, np.cos(angle), np.sin(angle))
    norm = np.where(freq == 0, 1.0, 2.0) / window
    return basis, freq, norm


@functools.cache
def tables(window):
    basis, freq, norm = real_basis(window)
    count = freq.size
    rows = -(-count // 16) * 16
    columns = np.zeros((window, window))
    columns[:, :count] = basis
    radius = (freq[:, None] ** 2 + freq[None, :] ** 2).astype(np.float64)
    weight = (9.0 * radius < window * window) * norm[:, None] * norm[None, :]
    angle = -PROPAGATION_COEF * (65536.0 / (window * window)) * radius
    prop = np.zeros((2, rows, window), np.float32)
    prop[0, :count, :count] = weight * np.cos(angle)
    prop[1, :count, :count] = weight * np.sin(angle)
    k = np.arange(window)
    f = np.where(k < window // 2, k, k - window)
    radius = (f[:, None] ** 2 + f[None, :] ** 2).astype(np.float64)
    inside = 16.0 * radius < window * window
    start = inside * (window / math.sqrt(inside.sum())) * np.exp(-1j * (DEFOCUS_COEF / window) * radius)
    wave = np.fft.ifft2(start) * window
    square = np.stack([columns, columns.T, wave.real, wave.imag]).astype(ml_dtypes.bfloat16)
    return square, prop


@functools.cache
def half_angle_coefs():
    nodes = 0.25 * (1.0 + np.cos(np.pi * (np.arange(400) + 0.5) / 400)) / 2.0
    f = np.sqrt(nodes)
    sin = np.polynomial.Polynomial.fit(nodes, math.sqrt(2.0) * np.sin(np.pi * f) / f, 4, domain=[0, 0.25], window=[0, 0.25]).coef
    cos = np.polynomial.Polynomial.fit(nodes, math.sqrt(2.0) * np.cos(np.pi * f), 4, domain=[0, 0.25], window=[0, 0.25]).coef
    return [float(c) for c in sin], [float(c) for c in cos]


def horner(coefs, z):
    total = coefs[-1]
    for c in coefs[-2::-1]:
        total = total * z + c
    return total


def cos_sin(phase):
    sin_coefs, cos_coefs = half_angle_coefs()
    turn = phase * (0.5 / math.pi)
    turn = turn - jnp.round(turn)
    z = turn * turn
    s = turn * horner(sin_coefs, z)
    c = horner(cos_coefs, z)
    return 1.0 - s * s, s * c


def dot(a, b):
    return jnp.dot(a, b, preferred_element_type=jnp.float32)


def kernel(
    n_lat, n_slc, window, field,
    xy_ref, species_ref, slab_ref, amp_ref, spread_ref, pos_ref, square_hbm, prop_hbm,
    out_ref,
    mine, recv, square, prop, table_sem, send_sem, recv_sem,
):
    bf16, f32 = jnp.bfloat16, jnp.float32
    t, u = lax.axis_index("lat"), lax.axis_index("slc")
    before, after = lax.rem(t + n_lat - 1, n_lat), lax.rem(t + 1, n_lat)
    owners = [lax.rem(u + n_slc - k, n_slc) for k in range(n_slc)]

    barrier = pltpu.get_barrier_semaphore()
    for k in range(n_slc):
        for lat in (before, after) if k == 0 else (before, after, t):
            pl.semaphore_signal(
                barrier, inc=1, device_id={"lat": lat, "slc": owners[k]}, device_id_type=MESH
            )
    loads = [
        pltpu.make_async_copy(square_hbm, square, table_sem.at[0]),
        pltpu.make_async_copy(prop_hbm, prop, table_sem.at[1]),
    ]
    for load in loads:
        load.start()

    species = species_ref[0]
    slab = slab_ref[0]
    amp = jnp.zeros(species.shape, f32)
    spread = jnp.ones(species.shape, f32)
    for i in range(amp_ref.shape[0]):
        amp = jnp.where(species == i, amp_ref[i], amp)
        spread = jnp.where(species == i, spread_ref[i], spread)
    layers = 2
    factor = (-0.5 * LOG2E) / (spread * spread)
    fields = [xy_ref[0, 0, 0:1, :], xy_ref[0, 0, 1:2, :], factor]
    fields += [jnp.where(slab == s, amp, 0.0) for s in range(layers)]
    for row, value in enumerate(fields):
        for h in range(2):
            mine[h, row : row + 1, :] = value[:, h * LANES : (h + 1) * LANES]
    for h in range(2):
        mine[h, len(fields) :, :] = jnp.zeros((8 - len(fields), LANES), f32)

    pl.semaphore_wait(barrier, 3 * n_slc - 1)
    sends = {}
    for k in range(n_slc):
        pieces = [(after, mine.at[1], recv.at[k, 0]), (before, mine.at[0], recv.at[k, 3])]
        if k > 0:
            pieces.append((t, mine, recv.at[k, 1:3]))
        for i, (lat, source, target) in enumerate(pieces):
            copy = pltpu.make_async_remote_copy(
                src_ref=source, dst_ref=target,
                send_sem=send_sem.at[k, i], recv_sem=recv_sem.at[k, i],
                device_id={"lat": lat, "slc": owners[k]}, device_id_type=MESH,
            )
            copy.start()
            sends[k, i] = copy
    for load in loads:
        load.wait()

    probes = pos_ref.shape[0]
    anchor_x = pos_ref[0, 0].astype(f32)
    anchor_y = [pos_ref[p, 1].astype(f32) for p in range(probes)]
    pixel = lax.broadcasted_iota(jnp.int32, (window, LANES), 0).astype(f32)
    half = 0.5 * window
    rows = prop.shape[1]
    basis, basis_t = square.at[0], square.at[1]

    waves = [(square[2].astype(f32), square[3].astype(f32))] * probes
    for k in range(n_slc):
        for i in range(2 if k == 0 else 3):
            sends[k, i].wait_recv()
        groups = [recv[k, 0], mine[0], mine[1], recv[k, 3]] if k == 0 else [recv[k, g] for g in range(4)]
        atoms, rel_x = None, None
        for group in groups[::-1]:
            rel = group[0:1, :] - anchor_x
            rel = jnp.where(rel < -0.5 * field, rel + field, rel)
            rel = jnp.where(rel >= 0.5 * field, rel - field, rel)
            if atoms is None:
                atoms, rel_x = group, rel
            else:
                seen = jnp.logical_and(rel >= -half, rel < window + half)
                atoms = jnp.where(seen, group, atoms)
                rel_x = jnp.where(seen, rel, rel_x)
        factor = atoms[2:3, :]
        d = rel_x - pixel
        across = jnp.exp2(d * d * factor).astype(bf16)
        along = []
        for p in range(probes):
            rel_y = atoms[1:2, :] - anchor_y[p]
            rel_y = jnp.where(rel_y < 0.0, rel_y + window, rel_y)
            e = jnp.abs(rel_y - pixel)
            e = jnp.minimum(e, window - e)
            along.append(jnp.exp2(e * e * factor))
        for s in range(layers):
            last = k == n_slc - 1 and s == layers - 1
            for p in range(probes):
                weighted = (atoms[3 + s : 4 + s, :] * along[p]).astype(bf16)
                phase = lax.dot_general(
                    across, weighted, (((1,), (1,)), ((), ())), preferred_element_type=f32
                )
                c, sn = cos_sin(phase)
                re, im = waves[p]
                sent = [(re * c - im * sn).astype(bf16), (re * sn + im * c).astype(bf16)]
                rowwise = [dot(w, basis[...]).astype(bf16) for w in sent]
                sr, si = [dot(basis_t[:rows, :], w) for w in rowwise]
                pr, pi = prop[0], prop[1]
                spectrum = [(sr * pr - si * pi).astype(bf16), (sr * pi + si * pr).astype(bf16)]
                back = [dot(w, basis_t[...]).astype(bf16) for w in spectrum]
                pad = jnp.zeros((window - rows, window), bf16)
                back = [jnp.concatenate([w, pad], 0) for w in back]
                waves[p] = tuple(dot(basis[...], w) for w in back)
                if last:
                    for part in range(2):
                        out_ref[p, part] = waves[p][part].astype(bf16)
    for copy in sends.values():
        copy.wait_send()


def solution(mesh):
    n_lat, n_slc = mesh.shape["lat"], mesh.shape["slc"]
    window = 256

    def shards(atom_xy, atom_species, atom_slab, species_amp, species_spread, margin, probe_pos):
        square, prop = tables(window)
        atoms = atom_xy.shape[-1]
        field = float(n_lat * atoms * 4)
        probes = probe_pos.shape[0]
        vmem = pl.BlockSpec(memory_space=pltpu.VMEM)
        smem = pl.BlockSpec(memory_space=pltpu.SMEM)
        hbm = pl.BlockSpec(memory_space=pl.ANY)
        out = pl.pallas_call(
            functools.partial(kernel, n_lat, n_slc, window, field),
            out_shape=jax.ShapeDtypeStruct((probes, 2, window, window), jnp.bfloat16),
            in_specs=[vmem, vmem, vmem, smem, smem, smem, hbm, hbm],
            out_specs=vmem,
            scratch_shapes=[
                pltpu.VMEM((2, 8, LANES), jnp.float32),
                pltpu.VMEM((n_slc, 4, 8, LANES), jnp.float32),
                pltpu.VMEM(square.shape, jnp.bfloat16),
                pltpu.VMEM(prop.shape, jnp.float32),
                pltpu.SemaphoreType.DMA((2,)),
                pltpu.SemaphoreType.DMA((n_slc, 3)),
                pltpu.SemaphoreType.DMA((n_slc, 3)),
            ],
            compiler_params=pltpu.CompilerParams(
                collective_id=0, has_side_effects=True, vmem_limit_bytes=40 * 2**20
            ),
            name="multislice",
        )(atom_xy, atom_species, atom_slab, species_amp, species_spread, probe_pos,
          jnp.asarray(square), jnp.asarray(prop))
        return jnp.transpose(out, (0, 2, 1, 3))

    in_specs = (
        P(("groups", "lat"), "slc", None, None),
        P(("groups", "lat"), "slc", None),
        P(("groups", "lat"), "slc", None),
        P(),
        P(),
        P(("groups", "lat"), "slc", None, "rep", None, None),
        P(("groups", "lat", "slc", "rep"), None),
    )
    out_specs = P(("groups", "lat", "slc", "rep"), None, None, None)
    return jax.shard_map(shards, mesh=mesh, in_specs=in_specs, out_specs=out_specs, check_vma=False)
```

profile of v0, /device:TPU:0, one launch (start us, length us, event | category | flops | bytes accessed | tf_op | source)
XLA Modules:
  0.0 24.0 jit_solution(6857415813058709943)
XLA Ops:
  0.0 0.0 copy-start
  0.0 1.0 %copy-done = bf16[4,256,256]{2,1,0:T(8,128)(2,1)S(1)} copy-done((bf16[4,256,256]{2,1,0:T(8,128)(2,1)S(1)}, bf16[4,256,256]{2,1,0:T(8,128)(2,1)}, u32[]{:S(2)}) %copy-start) | copy-done | bytes 524312
  1.0 0.0 copy-start.1
  1.0 1.0 %copy-done.1 = f32[2,176,256]{2,1,0:T(8,128)S(1)} copy-done((f32[2,176,256]{2,1,0:T(8,128)S(1)}, f32[2,176,256]{2,1,0:T(8,128)}, u32[]{:S(2)}) %copy-start.1) | copy-done | bytes 360472
  2.0 0.0 copy-start.2
  2.0 0.7 %copy-done.2 = f32[1,1,2,256]{3,2,1,0:T(2,128)S(1)} copy-done((f32[1,1,2,256]{3,2,1,0:T(2,128)S(1)}, f32[1,1,2,256]{3,2,1,0:T(2,128)}, u32[]{:S(2)}) %copy-start.2) | copy-done | bytes 2072
  2.7 0.0 copy-start.3
  2.7 0.7 %copy-done.3 = s32[1,1,256]{2,1,0:T(1,128)S(1)} copy-done((s32[1,1,256]{2,1,0:T(1,128)S(1)}, s32[1,1,256]{2,1,0:T(1,128)}, u32[]{:S(2)}) %copy-start.3) | copy-done | bytes 1048
  3.4 0.0 copy-start.4
  3.4 0.7 %copy-done.4 = s32[1,1,256]{2,1,0:T(1,128)S(1)} copy-done((s32[1,1,256]{2,1,0:T(1,128)S(1)}, s32[1,1,256]{2,1,0:T(1,128)}, u32[]{:S(2)}) %copy-start.4) | copy-done | bytes 1048
  4.1 0.0 copy-start.5
  4.1 0.7 %copy-done.5 = s32[2,2]{1,0:T(2,128)S(1)} copy-done((s32[2,2]{1,0:T(2,128)S(1)}, s32[2,2]{1,0:T(2,128)}, u32[]{:S(2)}) %copy-start.5) | copy-done | bytes 40
  4.7 0.0 copy-start.6
  4.8 0.7 %copy-done.6 = f32[8]{0:T(128)S(1)} copy-done((f32[8]{0:T(128)S(1)}, f32[8]{0:T(128)}, u32[]{:S(2)}) %copy-start.6) | copy-done | bytes 56
  5.4 0.0 copy-start.7
  5.4 0.7 %copy-done.7 = f32[8]{0:T(128)S(1)} copy-done((f32[8]{0:T(128)S(1)}, f32[8]{0:T(128)}, u32[]{:S(2)}) %copy-start.7) | copy-done | bytes 56
  6.1 16.6 %multislice.1 = bf16[2,2,256,256]{3,2,1,0:T(8,128)(2,1)S(1)} custom-call(f32[1,1,2,256]{3,2,1,0:T(2,128)S(1)} %copy-done.2, s32[1,1,256]{2,1,0:T(1,128)S(1)} %copy-done.3, s32[1,1,256]{2,1,0:T(1,128)S(1)} %copy-done.4, f32[8]{0:T(128)S(1)} %copy-done.6, f32[8]{0:T(128)S(1)} %copy-done.7, s32[2,2]{1,0:T(2,128)S(1)} %copy-done.5, ...), custom_call_target="tpu_custom_call" | custom-call | tf_op jit(solution)/shard_map/multislice/pallas_call | solution.py:213
  22.7 1.3 %copy.9 = bf16[2,256,2,256]{3,2,1,0:T(2,128)(2,1)} copy(bf16[2,256,2,256]{3,1,2,0:T(8,128)(2,1)S(1)} %bitcast.1) | data formatting | bytes 1048576 | tf_op jit(solution)/shard_map/transpose | solution.py:233
Async XLA Ops:
  0.0 1.0 %copy-start = (bf16[4,256,256]{2,1,0:T(8,128)(2,1)S(1)}, bf16[4,256,256]{2,1,0:T(8,128)(2,1)}, u32[]{:S(2)}) copy-start(bf16[4,256,256]{2,1,0:T(8,128)(2,1)} %constant.4.clone.square_hbm) | copy-start | bytes 1572868
  1.0 1.0 %copy-start.1 = (f32[2,176,256]{2,1,0:T(8,128)S(1)}, f32[2,176,256]{2,1,0:T(8,128)}, u32[]{:S(2)}) copy-start(f32[2,176,256]{2,1,0:T(8,128)} %constant.5.clone.prop_hbm) | copy-start | bytes 1081348
  2.0 0.7 %copy-start.2 = (f32[1,1,2,256]{3,2,1,0:T(2,128)S(1)}, f32[1,1,2,256]{3,2,1,0:T(2,128)}, u32[]{:S(2)}) copy-start(f32[1,1,2,256]{3,2,1,0:T(2,128)} %xy_ref.1) | copy-start | bytes 6148
  2.7 0.7 %copy-start.3 = (s32[1,1,256]{2,1,0:T(1,128)S(1)}, s32[1,1,256]{2,1,0:T(1,128)}, u32[]{:S(2)}) copy-start(s32[1,1,256]{2,1,0:T(1,128)} %species_ref.1) | copy-start | bytes 3076
  3.4 0.7 %copy-start.4 = (s32[1,1,256]{2,1,0:T(1,128)S(1)}, s32[1,1,256]{2,1,0:T(1,128)}, u32[]{:S(2)}) copy-start(s32[1,1,256]{2,1,0:T(1,128)} %slab_ref.1) | copy-start | bytes 3076
  4.1 0.7 %copy-start.5 = (s32[2,2]{1,0:T(2,128)S(1)}, s32[2,2]{1,0:T(2,128)}, u32[]{:S(2)}) copy-start(s32[2,2]{1,0:T(2,128)} %pos_ref.1) | copy-start | bytes 52
  4.7 0.7 %copy-start.6 = (f32[8]{0:T(128)S(1)}, f32[8]{0:T(128)}, u32[]{:S(2)}) copy-start(f32[8]{0:T(128)} %amp_ref.1) | copy-start | bytes 100
  5.4 0.7 %copy-start.7 = (f32[8]{0:T(128)S(1)}, f32[8]{0:T(128)}, u32[]{:S(2)}) copy-start(f32[8]{0:T(128)} %spread_ref.1) | copy-start | bytes 100
where the time goes:
time: 24.3 us; the launch traced here: 24 us
  Pallas kernels  16.6 us (68%)
  local copies, waits for them, and re-layouts  7.38 us (30%)
    pallas_call x1, Pallas kernels, shards(): pl.pallas_call(functools.partial(kernel, n_lat, n_slc, window, field), ou...  16.6 us
    unnamed x16, local copies, waits for them, and re-layouts  6.05 us
    transpose x1, local copies, waits for them, and re-layouts, shards(): return jnp.transpose(out, (0, 2, 1, 3))  1.33 us

commit v1 on v0

--- a/solution.py
+++ b/solution.py
@@ -16,6 +16,9 @@
 MESH = pl.DeviceIdType.MESH
 
 LANES = 128
+CHUNK = 64
+LAG = 4
+FILL = 1
 
 
 def real_basis(window):
@@ -83,9 +86,11 @@
 
 def kernel(
     n_lat, n_slc, window, field,
-    xy_ref, species_ref, slab_ref, amp_ref, spread_ref, pos_ref, square_hbm, prop_hbm,
+    xy_hbm, species_hbm, slab_hbm, amp_hbm, spread_hbm, pos_hbm, square_hbm, prop_hbm,
     out_ref,
-    mine, recv, square, prop, table_sem, send_sem, recv_sem,
+    xy_ref, species_ref, slab_ref, amp_ref, spread_ref, pos_ref, square, prop,
+    mine, recv, across, weighted, turn, sent, mixed, spectrum,
+    load_sem, send_sem, recv_sem,
 ):
     bf16, f32 = jnp.bfloat16, jnp.float32
     t, u = lax.axis_index("lat"), lax.axis_index("slc")
@@ -98,12 +103,15 @@
             pl.semaphore_signal(
                 barrier, inc=1, device_id={"lat": lat, "slc": owners[k]}, device_id_type=MESH
             )
-    loads = [
-        pltpu.make_async_copy(square_hbm, square, table_sem.at[0]),
-        pltpu.make_async_copy(prop_hbm, prop, table_sem.at[1]),
+    pairs = [
+        (xy_hbm, xy_ref), (species_hbm, species_ref), (slab_hbm, slab_ref), (amp_hbm, amp_ref),
+        (spread_hbm, spread_ref), (pos_hbm, pos_ref), (square_hbm, square), (prop_hbm, prop),
     ]
+    loads = [pltpu.make_async_copy(*pair, load_sem.at[i]) for i, pair in enumerate(pairs)]
     for load in loads:
         load.start()
+    for load in loads[:5]:
+        load.wait()
 
     species = species_ref[0]
     slab = slab_ref[0]
@@ -136,7 +144,7 @@
             )
             copy.start()
             sends[k, i] = copy
-    for load in loads:
+    for load in loads[5:]:
         load.wait()
 
     probes = pos_ref.shape[0]
@@ -146,9 +154,10 @@
     half = 0.5 * window
     rows = prop.shape[1]
     basis, basis_t = square.at[0], square.at[1]
-
-    waves = [(square[2].astype(f32), square[3].astype(f32))] * probes
-    for k in range(n_slc):
+    steps = n_slc * layers
+    done = {}
+
+    def owner_atoms(k):
         for i in range(2 if k == 0 else 3):
             sends[k, i].wait_recv()
         groups = [recv[k, 0], mine[0], mine[1], recv[k, 3]] if k == 0 else [recv[k, g] for g in range(4)]
@@ -163,37 +172,91 @@
                 seen = jnp.logical_and(rel >= -half, rel < window + half)
                 atoms = jnp.where(seen, group, atoms)
                 rel_x = jnp.where(seen, rel, rel_x)
-        factor = atoms[2:3, :]
-        d = rel_x - pixel
-        across = jnp.exp2(d * d * factor).astype(bf16)
-        along = []
-        for p in range(probes):
-            rel_y = atoms[1:2, :] - anchor_y[p]
-            rel_y = jnp.where(rel_y < 0.0, rel_y + window, rel_y)
-            e = jnp.abs(rel_y - pixel)
-            e = jnp.minimum(e, window - e)
-            along.append(jnp.exp2(e * e * factor))
-        for s in range(layers):
-            last = k == n_slc - 1 and s == layers - 1
+        return atoms, rel_x
+
+    def phases():
+        for k in range(n_slc):
+            atoms, rel_x = owner_atoms(k)
+            factor = atoms[2:3, :]
+            d = rel_x - pixel
+            across[...] = jnp.exp2(d * d * factor).astype(bf16)
             for p in range(probes):
-                weighted = (atoms[3 + s : 4 + s, :] * along[p]).astype(bf16)
-                phase = lax.dot_general(
-                    across, weighted, (((1,), (1,)), ((), ())), preferred_element_type=f32
-                )
-                c, sn = cos_sin(phase)
-                re, im = waves[p]
-                sent = [(re * c - im * sn).astype(bf16), (re * sn + im * c).astype(bf16)]
-                rowwise = [dot(w, basis[...]).astype(bf16) for w in sent]
-                sr, si = [dot(basis_t[:rows, :], w) for w in rowwise]
-                pr, pi = prop[0], prop[1]
-                spectrum = [(sr * pr - si * pi).astype(bf16), (sr * pi + si * pr).astype(bf16)]
-                back = [dot(w, basis_t[...]).astype(bf16) for w in spectrum]
-                pad = jnp.zeros((window - rows, window), bf16)
-                back = [jnp.concatenate([w, pad], 0) for w in back]
-                waves[p] = tuple(dot(basis[...], w) for w in back)
-                if last:
-                    for part in range(2):
-                        out_ref[p, part] = waves[p][part].astype(bf16)
+                rel_y = atoms[1:2, :] - anchor_y[p]
+                rel_y = jnp.where(rel_y < 0.0, rel_y + window, rel_y)
+                e = jnp.abs(rel_y - pixel)
+                e = jnp.minimum(e, window - e)
+                along = jnp.exp2(e * e * factor)
+                for s in range(layers):
+                    weighted[s, p] = (atoms[3 + s : 4 + s, :] * along).astype(bf16)
+            for s in range(layers):
+                for p in range(probes):
+                    phase = lax.dot_general(
+                        across[...], weighted[s, p], (((1,), (1,)), ((), ())), preferred_element_type=f32
+                    )
+                    step = k * layers + s
+                    for r in range(0, window, CHUNK):
+                        c, sn = cos_sin(phase[r : r + CHUNK])
+                        turn[step, p, 0, r : r + CHUNK, :] = c
+                        turn[step, p, 1, r : r + CHUNK, :] = sn
+                        if r + CHUNK == window:
+                            done[step, p] = True
+                        yield
+
+    blocks = [(r, min(96, rows - r)) for r in range(0, rows, 96)]
+
+    def chain(p):
+        wave = (square[2].astype(f32), square[3].astype(f32))
+        for step in range(steps):
+            yield step
+            for r in range(0, window, CHUNK):
+                part = slice(r, r + CHUNK)
+                re, im = wave[0][part], wave[1][part]
+                c, sn = turn[step, p, 0, part, :], turn[step, p, 1, part, :]
+                sent[p, 0, part, :] = (re * c - im * sn).astype(bf16)
+                sent[p, 1, part, :] = (re * sn + im * c).astype(bf16)
+            yield
+            for plane in range(2):
+                value = dot(basis_t[:rows, :], sent[p, plane]).astype(bf16)
+                for r, size in blocks:
+                    start = 2 * r + plane * size
+                    mixed[p, start : start + size, :] = value[r : r + size]
+                yield
+            for r, size in blocks:
+                both = dot(mixed[p, 2 * r : 2 * (r + size), :], basis[...])
+                sr, si = both[:size], both[size:]
+                pr, pi = prop[0, r : r + size, :], prop[1, r : r + size, :]
+                spectrum[p, r : r + size, :] = (sr * pr - si * pi).astype(bf16)
+                spectrum[p, rows + r : rows + r + size, :] = (sr * pi + si * pr).astype(bf16)
+                yield
+            back = dot(spectrum[p], basis_t[...]).astype(bf16)
+            yield
+            pad = jnp.zeros((window - rows, window), bf16)
+            wave = []
+            for plane in range(2):
+                full = jnp.concatenate([back[plane * rows : (plane + 1) * rows], pad], 0)
+                wave.append(dot(basis[...], full))
+                if step == steps - 1:
+                    out_ref[p, plane] = wave[plane].astype(bf16)
+                yield
+
+    filler = phases()
+    chains = [chain(p) for p in range(probes)]
+    at = [0] * probes
+    live = list(range(probes))
+    count = 0
+    while live:
+        for p in list(live):
+            if count < p * LAG:
+                continue
+            mark = next(chains[p], "end")
+            if mark == "end":
+                live.remove(p)
+            elif mark is not None:
+                while (mark, p) not in done:
+                    next(filler)
+            for _ in range(FILL):
+                next(filler, None)
+        count += 1
     for copy in sends.values():
         copy.wait_send()
 
@@ -208,24 +271,37 @@
         field = float(n_lat * atoms * 4)
         probes = probe_pos.shape[0]
         vmem = pl.BlockSpec(memory_space=pltpu.VMEM)
-        smem = pl.BlockSpec(memory_space=pltpu.SMEM)
-        hbm = pl.BlockSpec(memory_space=pl.ANY)
+        hbm = pl.BlockSpec(memory_space=pltpu.HBM)
+        rows = prop.shape[1]
+        layers = 2
         out = pl.pallas_call(
             functools.partial(kernel, n_lat, n_slc, window, field),
             out_shape=jax.ShapeDtypeStruct((probes, 2, window, window), jnp.bfloat16),
-            in_specs=[vmem, vmem, vmem, smem, smem, smem, hbm, hbm],
+            in_specs=[hbm] * 8,
             out_specs=vmem,
             scratch_shapes=[
+                pltpu.VMEM(atom_xy.shape, jnp.float32),
+                pltpu.VMEM(atom_species.shape, jnp.int32),
+                pltpu.VMEM(atom_slab.shape, jnp.int32),
+                pltpu.SMEM(species_amp.shape, jnp.float32),
+                pltpu.SMEM(species_spread.shape, jnp.float32),
+                pltpu.SMEM(probe_pos.shape, jnp.int32),
+                pltpu.VMEM(square.shape, jnp.bfloat16),
+                pltpu.VMEM(prop.shape, jnp.float32),
                 pltpu.VMEM((2, 8, LANES), jnp.float32),
                 pltpu.VMEM((n_slc, 4, 8, LANES), jnp.float32),
-                pltpu.VMEM(square.shape, jnp.bfloat16),
-                pltpu.VMEM(prop.shape, jnp.float32),
-                pltpu.SemaphoreType.DMA((2,)),
+                pltpu.VMEM((window, LANES), jnp.bfloat16),
+                pltpu.VMEM((layers, probes, window, LANES), jnp.bfloat16),
+                pltpu.VMEM((n_slc * layers, probes, 2, window, window), jnp.float32),
+                pltpu.VMEM((probes, 2, window, window), jnp.bfloat16),
+                pltpu.VMEM((probes, 2 * rows, window), jnp.bfloat16),
+                pltpu.VMEM((probes, 2 * rows, window), jnp.bfloat16),
+                pltpu.SemaphoreType.DMA((8,)),
                 pltpu.SemaphoreType.DMA((n_slc, 3)),
                 pltpu.SemaphoreType.DMA((n_slc, 3)),
             ],
             compiler_params=pltpu.CompilerParams(
-                collective_id=0, has_side_effects=True, vmem_limit_bytes=40 * 2**20
+                collective_id=0, has_side_effects=True, vmem_limit_bytes=63 * 2**20
             ),
             name="multislice",
         )(atom_xy, atom_species, atom_slab, species_amp, species_spread, probe_pos,

time: 24.3 us -> 16.7 us (0.69)
  local copies, waits for them, and re-layouts: 7.38 us -> 2.37 us
  Pallas kernels: 16.6 us -> 14.2 us
    unnamed x16 -> x0, local copies, waits for them, and re-layouts: 6.05 us -> none
    pallas_call x1, Pallas kernels: 16.6 us -> 14.2 us  [shards(): pl.pallas_call(functools.partial(kernel, n_lat, n_slc, window, field), ou...]
    transpose x1, local copies, waits for them, and re-layouts: 1.33 us -> 2.37 us  [shards(): return jnp.transpose(out, (0, 2, 1, 3))]
where the time goes in v1:
time: 16.7 us; the launch traced here: 16.5 us
  Pallas kernels  14.2 us (85%)
  local copies, waits for them, and re-layouts  2.37 us (14%)
    pallas_call x1, Pallas kernels, shards(): pl.pallas_call(functools.partial(kernel, n_lat, n_slc, window, field), ou...  14.2 us
    transpose x1, local copies, waits for them, and re-layouts, shards(): return jnp.transpose(out, (0, 2, 1, 3))  2.37 us

profile of v1, /device:TPU:0, one launch (start us, length us, event | category | flops | bytes accessed | tf_op | source)
XLA Modules:
  0.0 16.5 jit_solution(16495664487538786913)
XLA Ops:
  0.0 14.2 %multislice.1 = bf16[2,2,256,256]{3,2,1,0:T(8,128)(2,1)} custom-call(f32[1,1,2,256]{3,2,1,0:T(2,128)} %xy_hbm.1, s32[1,1,256]{2,1,0:T(1,128)} %species_hbm.1, s32[1,1,256]{2,1,0:T(1,128)} %slab_hbm.1, f32[8]{0:T(128)} %amp_hbm.1, f32[8]{0:T(128)} %spread_hbm.1, s32[2,2]{1,0:T(2,128)} %pos_hbm.1, bf16[4,256,256]{2,1,0:T(8,128)(2,1)} %constant.4.clone.square_hbm, ...), custom_call_target="tpu_custom_call" | custom-call | tf_op jit(solution)/shard_map/multislice/pallas_call | solution.py:277
  14.2 2.4 %copy.9 = bf16[2,256,2,256]{3,2,1,0:T(2,128)(2,1)} copy(bf16[2,256,2,256]{3,1,2,0:T(8,128)(2,1)} %bitcast.1) | data formatting | bytes 1048576 | tf_op jit(solution)/shard_map/transpose | solution.py:309

commit v2 on v1

--- a/solution.py
+++ b/solution.py
@@ -88,8 +88,8 @@
     n_lat, n_slc, window, field,
     xy_hbm, species_hbm, slab_hbm, amp_hbm, spread_hbm, pos_hbm, square_hbm, prop_hbm,
     out_ref,
-    xy_ref, species_ref, slab_ref, amp_ref, spread_ref, pos_ref, square, prop,
-    mine, recv, across, weighted, turn, sent, mixed, spectrum,
+    amp_ref, spread_ref, pos_ref, square, prop, xy_side, xy_mid, ids_side, ids_mid,
+    across, weighted, turn, sent, mixed, spectrum,
     load_sem, send_sem, recv_sem,
 ):
     bf16, f32 = jnp.bfloat16, jnp.float32
@@ -104,47 +104,36 @@
                 barrier, inc=1, device_id={"lat": lat, "slc": owners[k]}, device_id_type=MESH
             )
     pairs = [
-        (xy_hbm, xy_ref), (species_hbm, species_ref), (slab_hbm, slab_ref), (amp_hbm, amp_ref),
-        (spread_hbm, spread_ref), (pos_hbm, pos_ref), (square_hbm, square), (prop_hbm, prop),
+        (xy_hbm.at[0, 0], xy_mid.at[0]), (species_hbm.at[0], ids_mid.at[0, 0]),
+        (slab_hbm.at[0], ids_mid.at[0, 1]), (amp_hbm, amp_ref), (spread_hbm, spread_ref),
+        (pos_hbm, pos_ref), (square_hbm, square), (prop_hbm, prop),
     ]
     loads = [pltpu.make_async_copy(*pair, load_sem.at[i]) for i, pair in enumerate(pairs)]
     for load in loads:
         load.start()
-    for load in loads[:5]:
-        load.wait()
-
-    species = species_ref[0]
-    slab = slab_ref[0]
-    amp = jnp.zeros(species.shape, f32)
-    spread = jnp.ones(species.shape, f32)
-    for i in range(amp_ref.shape[0]):
-        amp = jnp.where(species == i, amp_ref[i], amp)
-        spread = jnp.where(species == i, spread_ref[i], spread)
+
     layers = 2
-    factor = (-0.5 * LOG2E) / (spread * spread)
-    fields = [xy_ref[0, 0, 0:1, :], xy_ref[0, 0, 1:2, :], factor]
-    fields += [jnp.where(slab == s, amp, 0.0) for s in range(layers)]
-    for row, value in enumerate(fields):
-        for h in range(2):
-            mine[h, row : row + 1, :] = value[:, h * LANES : (h + 1) * LANES]
-    for h in range(2):
-        mine[h, len(fields) :, :] = jnp.zeros((8 - len(fields), LANES), f32)
-
+    low, high = pl.ds(0, LANES), pl.ds(LANES, LANES)
     pl.semaphore_wait(barrier, 3 * n_slc - 1)
     sends = {}
     for k in range(n_slc):
-        pieces = [(after, mine.at[1], recv.at[k, 0]), (before, mine.at[0], recv.at[k, 3])]
-        if k > 0:
-            pieces.append((t, mine, recv.at[k, 1:3]))
-        for i, (lat, source, target) in enumerate(pieces):
-            copy = pltpu.make_async_remote_copy(
-                src_ref=source, dst_ref=target,
-                send_sem=send_sem.at[k, i], recv_sem=recv_sem.at[k, i],
-                device_id={"lat": lat, "slc": owners[k]}, device_id_type=MESH,
-            )
-            copy.start()
-            sends[k, i] = copy
-    for load in loads[5:]:
+        for side, (lat, part) in enumerate([(after, high), (before, low), (t, pl.ds(0, 2 * LANES))]):
+            if side == 2 and k == 0:
+                continue
+            if side < 2:
+                targets = [xy_side.at[k, side], ids_side.at[k, side, 0], ids_side.at[k, side, 1]]
+            else:
+                targets = [xy_mid.at[k], ids_mid.at[k, 0], ids_mid.at[k, 1]]
+            sources = [xy_hbm.at[0, 0, :, part], species_hbm.at[0, :, part], slab_hbm.at[0, :, part]]
+            for i in range(3):
+                copy = pltpu.make_async_remote_copy(
+                    src_ref=sources[i], dst_ref=targets[i],
+                    send_sem=send_sem.at[k, side, i], recv_sem=recv_sem.at[k, side, i],
+                    device_id={"lat": lat, "slc": owners[k]}, device_id_type=MESH,
+                )
+                copy.start()
+                sends[k, side, i] = copy
+    for load in loads:
         load.wait()
 
     probes = pos_ref.shape[0]
@@ -158,36 +147,50 @@
     done = {}
 
     def owner_atoms(k):
-        for i in range(2 if k == 0 else 3):
-            sends[k, i].wait_recv()
-        groups = [recv[k, 0], mine[0], mine[1], recv[k, 3]] if k == 0 else [recv[k, g] for g in range(4)]
+        for side in range(2 if k == 0 else 3):
+            for i in range(3):
+                sends[k, side, i].wait_recv()
+        ends = [
+            [xy_side[k, side, 0:1, :], xy_side[k, side, 1:2, :], ids_side[k, side, 0], ids_side[k, side, 1]]
+            for side in range(2)
+        ]
+        middle = [
+            [xy_mid[k, 0:1, h], xy_mid[k, 1:2, h], ids_mid[k, 0, :, h], ids_mid[k, 1, :, h]]
+            for h in (low, high)
+        ]
         atoms, rel_x = None, None
-        for group in groups[::-1]:
-            rel = group[0:1, :] - anchor_x
+        for group in [ends[1], middle[1], middle[0], ends[0]]:
+            rel = group[0] - anchor_x
             rel = jnp.where(rel < -0.5 * field, rel + field, rel)
             rel = jnp.where(rel >= 0.5 * field, rel - field, rel)
             if atoms is None:
-                atoms, rel_x = group, rel
+                atoms, rel_x = group[1:], rel
             else:
                 seen = jnp.logical_and(rel >= -half, rel < window + half)
-                atoms = jnp.where(seen, group, atoms)
+                atoms = [jnp.where(seen, new, old) for new, old in zip(group[1:], atoms)]
                 rel_x = jnp.where(seen, rel, rel_x)
-        return atoms, rel_x
+        y, species, slab = atoms
+        amp = jnp.zeros(species.shape, f32)
+        spread = jnp.ones(species.shape, f32)
+        for i in range(amp_ref.shape[0]):
+            amp = jnp.where(species == i, amp_ref[i], amp)
+            spread = jnp.where(species == i, spread_ref[i], spread)
+        factor = (-0.5 * LOG2E) / (spread * spread)
+        return rel_x, y, factor, [jnp.where(slab == s, amp, 0.0) for s in range(layers)]
 
     def phases():
         for k in range(n_slc):
-            atoms, rel_x = owner_atoms(k)
-            factor = atoms[2:3, :]
+            rel_x, y, factor, amps = owner_atoms(k)
             d = rel_x - pixel
             across[...] = jnp.exp2(d * d * factor).astype(bf16)
             for p in range(probes):
-                rel_y = atoms[1:2, :] - anchor_y[p]
+                rel_y = y - anchor_y[p]
                 rel_y = jnp.where(rel_y < 0.0, rel_y + window, rel_y)
                 e = jnp.abs(rel_y - pixel)
                 e = jnp.minimum(e, window - e)
                 along = jnp.exp2(e * e * factor)
                 for s in range(layers):
-                    weighted[s, p] = (atoms[3 + s : 4 + s, :] * along).astype(bf16)
+                    weighted[s, p] = (amps[s] * along).astype(bf16)
             for s in range(layers):
                 for p in range(probes):
                     phase = lax.dot_general(
@@ -276,20 +279,19 @@
         layers = 2
         out = pl.pallas_call(
             functools.partial(kernel, n_lat, n_slc, window, field),
-            out_shape=jax.ShapeDtypeStruct((probes, 2, window, window), jnp.bfloat16),
+            out_shape=pltpu.VMEM((probes, 2, window, window), jnp.bfloat16),
             in_specs=[hbm] * 8,
             out_specs=vmem,
             scratch_shapes=[
-                pltpu.VMEM(atom_xy.shape, jnp.float32),
-                pltpu.VMEM(atom_species.shape, jnp.int32),
-                pltpu.VMEM(atom_slab.shape, jnp.int32),
                 pltpu.SMEM(species_amp.shape, jnp.float32),
                 pltpu.SMEM(species_spread.shape, jnp.float32),
                 pltpu.SMEM(probe_pos.shape, jnp.int32),
                 pltpu.VMEM(square.shape, jnp.bfloat16),
                 pltpu.VMEM(prop.shape, jnp.float32),
-                pltpu.VMEM((2, 8, LANES), jnp.float32),
-                pltpu.VMEM((n_slc, 4, 8, LANES), jnp.float32),
+                pltpu.VMEM((n_slc, 2, 2, LANES), jnp.float32),
+                pltpu.VMEM((n_slc, 2, 2 * LANES), jnp.float32),
+                pltpu.VMEM((n_slc, 2, 2, 1, LANES), jnp.int32),
+                pltpu.VMEM((n_slc, 2, 1, 2 * LANES), jnp.int32),
                 pltpu.VMEM((window, LANES), jnp.bfloat16),
                 pltpu.VMEM((layers, probes, window, LANES), jnp.bfloat16),
                 pltpu.VMEM((n_slc * layers, probes, 2, window, window), jnp.float32),
@@ -297,11 +299,11 @@
                 pltpu.VMEM((probes, 2 * rows, window), jnp.bfloat16),
                 pltpu.VMEM((probes, 2 * rows, window), jnp.bfloat16),
                 pltpu.SemaphoreType.DMA((8,)),
-                pltpu.SemaphoreType.DMA((n_slc, 3)),
-                pltpu.SemaphoreType.DMA((n_slc, 3)),
+                pltpu.SemaphoreType.DMA((n_slc, 3, 3)),
+                pltpu.SemaphoreType.DMA((n_slc, 3, 3)),
             ],
             compiler_params=pltpu.CompilerParams(
-                collective_id=0, has_side_effects=True, vmem_limit_bytes=63 * 2**20
+                collective_id=0, has_side_effects=True, vmem_limit_bytes=int(63.4 * 2**20)
             ),
             name="multislice",
         )(atom_xy, atom_species, atom_slab, species_amp, species_spread, probe_pos,

time: 16.7 us -> 15.3 us (0.916)
  local copies, waits for them, and re-layouts: 2.37 us -> 1.33 us
  Pallas kernels: 14.2 us -> 13.8 us
    transpose x1, local copies, waits for them, and re-layouts: 2.37 us -> 1.33 us  [shards(): return jnp.transpose(out, (0, 2, 1, 3))]
    pallas_call x1, Pallas kernels: 14.2 us -> 13.8 us  [shards(): pl.pallas_call(functools.partial(kernel, n_lat, n_slc, window, field), ou...]
where the time goes in v2:
time: 15.3 us; the launch traced here: 15.1 us
  Pallas kernels  13.8 us (90%)
  local copies, waits for them, and re-layouts  1.33 us (9%)
    pallas_call x1, Pallas kernels, shards(): pl.pallas_call(functools.partial(kernel, n_lat, n_slc, window, field), ou...  13.8 us
    transpose x1, local copies, waits for them, and re-layouts, shards(): return jnp.transpose(out, (0, 2, 1, 3))  1.33 us

profile of v2, /device:TPU:0, one launch (start us, length us, event | category | flops | bytes accessed | tf_op | source)
XLA Modules:
  0.0 15.1 jit_solution(9276352859258771163)
XLA Ops:
  0.0 13.8 %multislice.1 = bf16[2,2,256,256]{3,2,1,0:T(8,128)(2,1)S(1)} custom-call(f32[1,1,2,256]{3,2,1,0:T(2,128)} %xy_hbm.1, s32[1,1,256]{2,1,0:T(1,128)} %species_hbm.1, s32[1,1,256]{2,1,0:T(1,128)} %slab_hbm.1, f32[8]{0:T(128)} %amp_hbm.1, f32[8]{0:T(128)} %spread_hbm.1, s32[2,2]{1,0:T(2,128)} %pos_hbm.1, bf16[4,256,256]{2,1,0:T(8,128)(2,1)} %constant.4.clone.square_hbm, ...), custom_call_target="tpu_custom_call" | custom-call | tf_op jit(solution)/shard_map/multislice/pallas_call | solution.py:280
  13.8 1.3 %copy.9 = bf16[2,256,2,256]{3,2,1,0:T(2,128)(2,1)} copy(bf16[2,256,2,256]{3,1,2,0:T(8,128)(2,1)S(1)} %bitcast.1) | data formatting | bytes 1048576 | tf_op jit(solution)/shard_map/transpose | solution.py:311

commit v3 on v2

--- a/solution.py
+++ b/solution.py
@@ -18,7 +18,7 @@
 LANES = 128
 CHUNK = 64
 LAG = 4
-FILL = 1
+PERIOD = 3
 
 
 def real_basis(window):
@@ -133,7 +133,7 @@
                 )
                 copy.start()
                 sends[k, side, i] = copy
-    for load in loads:
+    for load in loads[:6]:
         load.wait()
 
     probes = pos_ref.shape[0]
@@ -208,9 +208,13 @@
     blocks = [(r, min(96, rows - r)) for r in range(0, rows, 96)]
 
     def chain(p):
-        wave = (square[2].astype(f32), square[3].astype(f32))
         for step in range(steps):
             yield step
+            if step == 0:
+                if p == 0:
+                    for load in loads[6:]:
+                        load.wait()
+                wave = (square[2].astype(f32), square[3].astype(f32))
             for r in range(0, window, CHUNK):
                 part = slice(r, r + CHUNK)
                 re, im = wave[0][part], wave[1][part]
@@ -244,9 +248,8 @@
 
     filler = phases()
     chains = [chain(p) for p in range(probes)]
-    at = [0] * probes
     live = list(range(probes))
-    count = 0
+    count = parts = 0
     while live:
         for p in list(live):
             if count < p * LAG:
@@ -257,7 +260,8 @@
             elif mark is not None:
                 while (mark, p) not in done:
                     next(filler)
-            for _ in range(FILL):
+            parts += 1
+            if parts % PERIOD == 0:
                 next(filler, None)
         count += 1
     for copy in sends.values():

time: 15.3 us -> 15.1 us (0.987)
  Pallas kernels: 13.8 us -> 13.6 us
    pallas_call x1, Pallas kernels: 13.8 us -> 13.6 us  [shards(): pl.pallas_call(functools.partial(kernel, n_lat, n_slc, window, field), ou...]
where the time goes in v3:
time: 15.1 us; the launch traced here: 15 us
  Pallas kernels  13.6 us (90%)
  local copies, waits for them, and re-layouts  1.33 us (9%)
    pallas_call x1, Pallas kernels, shards(): pl.pallas_call(functools.partial(kernel, n_lat, n_slc, window, field), ou...  13.6 us
    transpose x1, local copies, waits for them, and re-layouts, shards(): return jnp.transpose(out, (0, 2, 1, 3))  1.33 us

profile of v3, /device:TPU:0, one launch (start us, length us, event | category | flops | bytes accessed | tf_op | source)
XLA Modules:
  0.0 15.0 jit_solution(14731181821294464129)
XLA Ops:
  0.0 13.6 %multislice.1 = bf16[2,2,256,256]{3,2,1,0:T(8,128)(2,1)S(1)} custom-call(f32[1,1,2,256]{3,2,1,0:T(2,128)} %xy_hbm.1, s32[1,1,256]{2,1,0:T(1,128)} %species_hbm.1, s32[1,1,256]{2,1,0:T(1,128)} %slab_hbm.1, f32[8]{0:T(128)} %amp_hbm.1, f32[8]{0:T(128)} %spread_hbm.1, s32[2,2]{1,0:T(2,128)} %pos_hbm.1, bf16[4,256,256]{2,1,0:T(8,128)(2,1)} %constant.4.clone.square_hbm, ...), custom_call_target="tpu_custom_call" | custom-call | tf_op jit(solution)/shard_map/multislice/pallas_call | solution.py:284
  13.6 1.3 %copy.9 = bf16[2,256,2,256]{3,2,1,0:T(2,128)(2,1)} copy(bf16[2,256,2,256]{3,1,2,0:T(8,128)(2,1)S(1)} %bitcast.1) | data formatting | bytes 1048576 | tf_op jit(solution)/shard_map/transpose | solution.py:315
